TPU v7x, 512 devices: a whole 4x8x8 slice. The times are simulated.
512 devices in a mesh: dp: 32 (over y, x_hi, core), mp: 16 (over x_lo, z).
Axes of the slice: x: 4 (x_hi: 2, x_lo: 2; x = x_hi * 2 + x_lo), y: 8, z: 8, core: 2. Of those that a mesh axis runs over, the one named last changes fastest.
Arguments:
- activations: bfloat16 [4096, 3072], P('dp', 'mp'), may hold values from -45 to 45
- cotangent: bfloat16 [4096, 3072], P('dp', 'mp'), may hold values from -6 to 6
- ln_gain: bfloat16 [3072], P('mp'), may hold values from 0.099609375 to 1.8984375
- w_in: bfloat16 [3072, 8192], P('dp', 'mp'), may hold values from -1 to 1
- w_out: bfloat16 [4096, 3072], P('mp'), may hold values from -0.09375 to 0.09375
- q_gain: bfloat16 [16, 128], P('mp'), may hold values from 0.5 to 4
- k_gain: bfloat16 [16, 128], P('mp'), may hold values from 0.5 to 4
Outputs:
- grad_x: bfloat16 [4096, 3072], P('dp', 'mp')
- grad_w_in: bfloat16 [3072, 8192], P('dp', 'mp')
- grad_w_out: bfloat16 [4096, 3072], P('mp')
- grad_ln_gain: float32 [3072], P('mp')
- grad_q_gain: float32 [16, 128], P('mp')
- grad_k_gain: float32 [16, 128], P('mp')
All inputs are finite; a program needn't handle non-finite values.
Results may differ from a plain program's by a relative error of at most 0.03.
Values may be sent and summed in bfloat16 or wider, within the bound.
A program may use at most 64 MiB of HBM per device.

v0:
```python
import jax
import jax.numpy as jnp
from jax import lax
from jax.sharding import PartitionSpec as P

PATCHES = 128


epsilon = 1e-06


def normalize(values):
    row_mean = jnp.mean(values, axis=-1, keepdims=True)
    centred = values - row_mean
    inv_std = lax.rsqrt(jnp.mean(centred * centred, axis=-1, keepdims=True) + epsilon)
    return (centred * inv_std, inv_std)


def norm_back(grad_hat, x_hat, inv_std):
    mean_grad = jnp.mean(grad_hat, axis=-1, keepdims=True)
    mean_cross = jnp.mean(grad_hat * x_hat, axis=-1, keepdims=True)
    return inv_std * (grad_hat - mean_grad - x_hat * mean_cross)


def gelu_pair(pre_act):
    normal_cdf = 0.5 * (1.0 + lax.erf(pre_act * 0.7071067811865476))
    normal_pdf = jnp.exp(-0.5 * pre_act * pre_act) * 0.3989422804014327
    return (pre_act * normal_cdf, normal_cdf + pre_act * normal_pdf)


def attend(q_raw, k_raw, v_raw, grad_out, q_gain, k_gain):
    scaling = q_raw.shape[-1] ** (-0.5)
    q_hat, q_inv = normalize(q_raw)
    k_hat, k_inv = normalize(k_raw)
    q_normed = (q_hat * q_gain.astype(jnp.float32)).astype(jnp.bfloat16)
    k_normed = (k_hat * k_gain.astype(jnp.float32)).astype(jnp.bfloat16)
    v_bf = v_raw.astype(jnp.bfloat16)
    scores = (
        jnp.einsum("ipgd,iqgd->igpq", q_normed, k_normed, preferred_element_type=jnp.float32)
        * scaling
    )
    attn_prob = jax.nn.softmax(scores, axis=-1)
    prob_bf = attn_prob.astype(jnp.bfloat16)
    out_bf = jnp.einsum(
        "igpq,iqgd->ipgd", prob_bf, v_bf, preferred_element_type=jnp.float32
    ).astype(jnp.bfloat16)
    grad_prob = jnp.einsum("ipgd,iqgd->igpq", grad_out, v_bf, preferred_element_type=jnp.float32)
    grad_v = jnp.einsum("igpq,ipgd->iqgd", prob_bf, grad_out, preferred_element_type=jnp.float32)
    grad_score = (
        attn_prob * (grad_prob - jnp.sum(attn_prob * grad_prob, axis=-1, keepdims=True)) * scaling
    ).astype(jnp.bfloat16)
    grad_qn = jnp.einsum(
        "igpq,iqgd->ipgd", grad_score, k_normed, preferred_element_type=jnp.float32
    )
    grad_kn = jnp.einsum(
        "igpq,ipgd->iqgd", grad_score, q_normed, preferred_element_type=jnp.float32
    )
    q_gain_grad = jnp.sum(grad_qn * q_hat, axis=(0, 1))
    k_gain_grad = jnp.sum(grad_kn * k_hat, axis=(0, 1))
    grad_q = norm_back(grad_qn * q_gain.astype(jnp.float32), q_hat, q_inv)
    grad_k = norm_back(grad_kn * k_gain.astype(jnp.float32), k_hat, k_inv)
    return (out_bf, grad_q, grad_k, grad_v, q_gain_grad, k_gain_grad)


def per_device(activations, cotangent, ln_gain, w_in, w_out, q_gain, k_gain):
    heads_here = q_gain.shape[0]
    head_dim = q_gain.shape[1]
    head_width = heads_here * head_dim
    tokens = activations.shape[0]
    images = tokens // PATCHES
    width_here = activations.shape[1]
    replicas = lax.axis_size("dp")

    def as_heads(block):
        return block.reshape(images, PATCHES, heads_here, head_dim)

    x_full, gain_full = (
        lax.all_gather(activations, "mp", axis=1, tiled=True),
        lax.all_gather(ln_gain, "mp", axis=0, tiled=True),
    )
    x_hat, x_inv = normalize(x_full.astype(jnp.float32))
    x_normed = (x_hat * gain_full.astype(jnp.float32)).astype(jnp.bfloat16)
    w_full = lax.all_gather(w_in, "dp", axis=0, tiled=True)
    projected = jnp.dot(x_normed, w_full, preferred_element_type=jnp.float32)
    dy_full = lax.all_gather(cotangent, "mp", axis=1, tiled=True)
    grad_cat = lax.dot_general(
        dy_full, w_out, (((1,), (1,)), ((), ())), preferred_element_type=jnp.float32
    )
    activation, gelu_slope = gelu_pair(projected[:, 3 * head_width :])
    act_bf = activation.astype(jnp.bfloat16)
    grad_out_bf = as_heads(grad_cat[:, :head_width].astype(jnp.bfloat16))
    out_bf, grad_q, grad_k, grad_v, q_gain_grad, k_gain_grad = attend(
        as_heads(projected[:, :head_width]),
        as_heads(projected[:, head_width : 2 * head_width]),
        as_heads(projected[:, 2 * head_width : 3 * head_width]),
        grad_out_bf,
        q_gain,
        k_gain,
    )
    joined = jnp.concatenate([out_bf.reshape(tokens, head_width), act_bf], axis=1)
    out_term = lax.dot_general(
        joined, dy_full, (((0,), (0,)), ((), ())), preferred_element_type=jnp.float32
    )
    out_sum = lax.psum(out_term.astype(jnp.bfloat16), "dp").astype(jnp.float32)
    grad_pre = grad_cat[:, head_width:] * gelu_slope
    grad_proj = jnp.concatenate(
        [
            grad_q.reshape(tokens, head_width),
            grad_k.reshape(tokens, head_width),
            grad_v.reshape(tokens, head_width),
            grad_pre,
        ],
        axis=1,
    ).astype(jnp.bfloat16)
    in_sum = lax.psum_scatter(
        lax.dot_general(
            x_normed, grad_proj, (((0,), (0,)), ((), ())), preferred_element_type=jnp.float32
        ).astype(jnp.bfloat16),
        "dp",
        scatter_dimension=0,
        tiled=True,
    ).astype(jnp.float32)
    dxn_term = lax.dot_general(
        grad_proj, w_full, (((1,), (1,)), ((), ())), preferred_element_type=jnp.float32
    )
    col_start = lax.axis_index("mp") * width_here
    hat_here = lax.dynamic_slice_in_dim(x_hat, col_start, width_here, 1)
    gain_here = ln_gain.astype(jnp.float32)
    full_width = gain_full.shape[0]
    dxn_here = lax.psum_scatter(
        dxn_term.astype(jnp.bfloat16), "mp", scatter_dimension=1, tiled=True
    ).astype(jnp.float32)
    scaled = dxn_here * gain_here
    sum_grad, sum_cross = lax.psum(
        (jnp.sum(scaled, axis=1, keepdims=True), jnp.sum(scaled * hat_here, axis=1, keepdims=True)),
        "mp",
    )
    mean_grad = sum_grad / full_width
    mean_cross = sum_cross / full_width
    grad_x = (
        cotangent.astype(jnp.float32) + x_inv * (scaled - mean_grad - hat_here * mean_cross)
    ).astype(jnp.bfloat16)
    ln_term = jnp.sum(dxn_here * hat_here, axis=0)
    ln_sum, q_sum, k_sum = lax.psum((ln_term, q_gain_grad, k_gain_grad), "dp")
    factor = 1.0 / replicas
    return (
        grad_x,
        (in_sum * factor).astype(jnp.bfloat16),
        (out_sum * factor).astype(jnp.bfloat16),
        ln_sum * factor,
        q_sum * factor,
        k_sum * factor,
    )


def solution(mesh):
    in_specs = (
        P("dp", "mp"),
        P("dp", "mp"),
        P("mp"),
        P("dp", "mp"),
        P("mp", None),
        P("mp", None),
        P("mp", None),
    )
    out_specs = (P("dp", "mp"), P("dp", "mp"), P("mp", None), P("mp"), P("mp", None), P("mp", None))
    return jax.shard_map(
        per_device, mesh=mesh, in_specs=in_specs, out_specs=out_specs, check_vma=False
    )
```

profile of v0, /device:TPU:1, one launch (start us, length us, event | category | flops | bytes accessed | tf_op | source)
XLA Modules:
  0.0 621.2 jit_solution(4001956487165084656)
XLA Ops:
  8.0 1.3 dynamic-slice
  10.8 34.8 %all-reduce = bf16[3072]{0:T(1024)(128)(2,1)S(1)} all-reduce(bf16[3072]{0:T(1024)(128)(2,1)S(1)} %dynamic-update-slice), channel_id=1, replica_groups=mesh['dp'=32,'mp'=16] {'mp'}, use_global_device_ids=true, to_apply=%add | all-reduce | flops 3072 | bytes 12288
  45.6 27.9 %all_gather.12 = bf16[128,3072]{0,1:T(8,128)(2,1)S(1)} all-gather(bf16[128,192]{0,1:T(8,128)(2,1)} %param.7), channel_id=1, replica_groups=mesh['dp'=32,'mp'=16] {'mp'}, dimensions={1}, use_global_device_ids=true | all-gather | bytes 835584 | tf_op jit(solution)/shard_map/all_gather | solution.py:78
  74.4 29.2 %all_gather.15 = bf16[128,3072]{0,1:T(8,128)(2,1)S(1)} all-gather(bf16[128,192]{0,1:T(8,128)(2,1)S(1)} %copy-done.4), channel_id=1, replica_groups=mesh['dp'=32,'mp'=16] {'mp'}, dimensions={1}, use_global_device_ids=true | all-gather | bytes 835584 | tf_op jit(solution)/shard_map/all_gather | solution.py:85
  103.6 1.3 fusion.51
  104.9 3.5 all-gather.2.cloned.1.call-done
  108.4 3.3 fusion.5
  113.3 0.9 convolution_bitcast_fusion.1
  114.2 1.7 fusion.27
  115.9 0.9 fusion.36
  116.9 1.9 convolution_convert_fusion.2
  118.9 1.1 fusion.3
  120.0 2.5 convolution_convert_fusion.1
  122.6 2.7 convolution_convert_fusion
  126.0 1.3 fusion
  127.3 67.5 %reduce-scatter.3.cloned.1.call-done = bf16[128,192]{0,1:T(8,128)(2,1)} async-done(((bf16[128,3072]{0,1:T(8,128)(2,1)}), bf16[128,192]{0,1:T(8,128)(2,1)}) %reduce-scatter.3.cloned.1.call-update) | async-done | bytes 49168 | tf_op jit(solution)/shard_map/reduce_scatter | solution.py:130
  194.8 1.1 fusion.14
  195.8 26.2 %all-reduce.2 = (f32[128,1]{0,1:T(1,128)S(1)}, f32[128,1]{0,1:T(1,128)S(1)}) all-reduce(f32[128,1]{0,1:T(1,128)S(1)} %bitcast.76, f32[128,1]{0,1:T(1,128)S(1)} %bitcast.77), channel_id=1, replica_groups=mesh['dp'=32,'mp'=16] {'mp'}, use_global_device_ids=true, to_apply=%region_17.0 | all-reduce | flops 256 | bytes 2048 | tf_op jit(solution)/shard_map/psum | solution.py:134
  222.1 82.1 %all-reduce.1 = (f32[192]{0:T(256)S(1)}, f32[1,128]{1,0:T(1,128)S(1)}, f32[1,128]{1,0:T(1,128)S(1)}) all-reduce(f32[192]{0:T(256)S(1)} %get-tuple-element.6, f32[1,128]{1,0:T(1,128)S(1)} %bitcast.79, f32[1,128]{1,0:T(1,128)S(1)} %bitcast.78), channel_id=1, replica_groups=mesh['dp'=32,'mp'=16] {'dp'}, use_global_device_ids=true, to_apply=%region_21.0 | all-reduce | flops 448 | bytes 3584 | tf_op jit(solution)/shard_map/psum | solution.py:144
  305.7 1.6 fusion.12
  307.4 175.4 %all-reduce.5.cloned.1.call-done = bf16[256,3072]{1,0:T(8,128)(2,1)} async-done(((bf16[256,3072]{1,0:T(8,128)(2,1)}), bf16[256,3072]{1,0:T(8,128)(2,1)}) %all-reduce.5.cloned.1.call-update) | async-done | bytes 1572880 | tf_op jit(solution)/shard_map/psum | solution.py:104
  482.8 2.9 multiply_convert_fusion
  485.6 127.5 %reduce-scatter.5.cloned.1.call-done = bf16[96,512]{1,0:T(8,128)(2,1)} async-done(((bf16[3072,512]{1,0:T(8,128)(2,1)}), bf16[96,512]{1,0:T(8,128)(2,1)}) %reduce-scatter.5.cloned.1.call-update) | async-done | bytes 98320 | tf_op jit(solution)/shard_map/reduce_scatter | solution.py:115
  613.1 1.6 multiply_convert_fusion.2
  (80 shorter events, 6.5 us)
Async XLA Ops:
  7.2 96.4 %copy-start = (bf16[256,3072]{1,0:T(8,128)(2,1)S(1)}, bf16[256,3072]{1,0:T(8,128)(2,1)}, u32[]{:S(2)}) copy-start(bf16[256,3072]{1,0:T(8,128)(2,1)} %param.11) | copy-start | bytes 4718596
  7.2 67.2 %copy-start.17 = (bf16[1,128]{1,0:T(2,128)(2,1)S(1)}, bf16[1,128]{1,0:T(2,128)(2,1)}, u32[]{:S(2)}) copy-start(bf16[1,128]{1,0:T(2,128)(2,1)} %param.13) | copy-start | bytes 772
  7.2 67.2 %copy-start.18 = (bf16[1,128]{1,0:T(2,128)(2,1)S(1)}, bf16[1,128]{1,0:T(2,128)(2,1)}, u32[]{:S(2)}) copy-start(bf16[1,128]{1,0:T(2,128)(2,1)} %param.12) | copy-start | bytes 772
  7.2 67.2 %copy-start.4 = (bf16[128,192]{0,1:T(8,128)(2,1)S(1)}, bf16[128,192]{0,1:T(8,128)(2,1)}, u32[]{:S(2)}) copy-start(bf16[128,192]{0,1:T(8,128)(2,1)} %param.8) | copy-start | bytes 147460
  7.2 101.1 %all-gather.2.cloned.1.call-start = ((), (), s32[]{:S(2)}) async-start(), calls=%async_computation.2 | async-start | bytes 3244032 | tf_op jit(solution)/shard_map/all_gather | solution.py:83
  7.9 186.8 %reduce-scatter.3.cloned.1.call-start = ((), (), s32[]{:S(2)}) async-start(), calls=%async_computation.3 | async-start | bytes 835584 | tf_op jit(solution)/shard_map/reduce_scatter | solution.py:130
  45.6 62.7 %copy-start.7 = (f32[3072]{0:T(1024)}, f32[3072]{0:T(1024)S(1)}, u32[]{:S(2)}) copy-start(f32[3072]{0:T(1024)S(1)} %convert_element_type.80) | copy-start | bytes 36868
  73.9 34.5 %copy-start.11 = (f32[128]{0:T(128)}, f32[128]{0:T(128)S(1)}, u32[]{:S(2)}) copy-start(f32[128]{0:T(128)S(1)} %broadcast_multiply_fusion.9) | copy-start | bytes 1540
  74.4 34.0 %copy-start.9 = (f32[128]{0:T(128)}, f32[128]{0:T(128)S(1)}, u32[]{:S(2)}) copy-start(f32[128]{0:T(128)S(1)} %add_rsqrt_fusion.2) | copy-start | bytes 1540
  74.4 38.2 %copy-start.15 = (f32[128]{0:T(128)}, f32[128]{0:T(128)S(1)}, u32[]{:S(2)}) copy-start(f32[128]{0:T(128)S(1)} %get-tuple-element.39) | copy-start | bytes 1540
  74.4 38.2 %copy-start.16 = (f32[128]{0:T(128)}, f32[128]{0:T(128)S(1)}, u32[]{:S(2)}) copy-start(f32[128]{0:T(128)S(1)} %get-tuple-element.40) | copy-start | bytes 1540
  108.4 3.5 copy-start.2
  108.4 8.5 %copy-start.1 = (bf16[3072,512]{1,0:T(8,128)(2,1)S(1)}, bf16[3072,512]{1,0:T(8,128)(2,1)}, u32[]{:S(2)}) copy-start(bf16[3072,512]{1,0:T(8,128)(2,1)} %all-gather.2.cloned.1.call-done) | copy-start | bytes 9437188
  112.9 3.0 copy-start.3
  112.9 4.0 copy-start.13
  113.0 3.9 copy-start.14
  113.1 3.8 copy-start.5
  118.8 364.0 %all-reduce.5.cloned.1.call-start = ((), (), s32[]{:S(2)}) async-start(), calls=%async_computation.5 | async-start | bytes 3145728 | tf_op jit(solution)/shard_map/psum | solution.py:104
  119.9 2.6 copy-start.6
  119.9 2.6 copy-start.8
  119.9 2.6 copy-start.10
  122.5 490.6 %reduce-scatter.5.cloned.1.call-start = ((), (), s32[]{:S(2)}) async-start(), calls=%async_computation.4 | async-start | bytes 3244032 | tf_op jit(solution)/shard_map/reduce_scatter | solution.py:115
  126.0 96.1 %copy-start.19 = (f32[128]{0:T(128)S(1)}, f32[128]{0:T(128)}, u32[]{:S(2)}) copy-start(f32[128]{0:T(128)} %get-tuple-element.8) | copy-start | bytes 1540
  126.0 96.1 %copy-start.20 = (f32[128]{0:T(128)S(1)}, f32[128]{0:T(128)}, u32[]{:S(2)}) copy-start(f32[128]{0:T(128)} %get-tuple-element.13) | copy-start | bytes 1540
  (2 other events, 3.3 us)
Sparse Core Ops, SparseCore 0:
  11.4 96.8 all-gather.1
  118.9 75.7 reduce-scatter.2
  197.9 284.7 all-reduce.4
  487.4 125.7 reduce-scatter.4
where the time goes:
time: 626 us; the launch traced here: 621 us
  waiting for transfers between devices  375 us (60%)
  blocking collectives  200 us (32%)
  matrix products  16 us (3%)
  between operations  14.8 us (2%)
  other arithmetic  12.8 us (2%)
    psum x1, waiting for transfers between devices, per_device(): out_sum = lax.psum(out_term.astype(jnp.bfloat16), 'dp').astype(jnp.float32)  175 us
    reduce_scatter x1, waiting for transfers between devices, per_device(): lax.psum_scatter(lax.dot_general(x_normed, grad_proj, (((0,), (0,)), ((),...  127 us
    psum x1, blocking collectives, per_device(): ln_sum, q_sum, k_sum = lax.psum((ln_term, q_gain_grad, k_gain_grad), 'dp')  82.1 us
    reduce_scatter x1, waiting for transfers between devices, per_device(): lax.psum_scatter(dxn_term.astype(jnp.bfloat16), 'mp', scatter_dimension=1...  67.5 us
    unnamed x1, blocking collectives  34.8 us
    all_gather x1, blocking collectives, per_device(): dy_full = lax.all_gather(cotangent, 'mp', axis=1, tiled=True)  29.2 us
    all_gather x1, blocking collectives, per_device(): lax.all_gather(activations, 'mp', axis=1, tiled=True)  27.9 us
    psum x1, blocking collectives, per_device(): lax.psum((jnp.sum(scaled, axis=1, keepdims=True), jnp.sum(scaled * hat_he...  26.2 us
  transfers between devices with their start and end apart: 4, of which 4 were waited for; matrix products, arithmetic and copies ran while one was open for 3% of the time, Pallas kernels for 0%

commit v1 on v0

v1 whole, which is shorter than its diff:
```python
import jax
import jax.numpy as jnp
from jax import lax
from jax.experimental import pallas as pl
from jax.experimental.pallas import tpu as pltpu
from jax.sharding import PartitionSpec as P

F32 = jnp.float32
BF16 = jnp.bfloat16
EPS = 1e-6
RING = 8
WIDTH = 3072
FACTOR = 1.0 / 32.0


def dot(a, b):
    return jnp.dot(a, b, preferred_element_type=F32)


def dot_t(a, b):
    return lax.dot_general(a, b, (((1,), (1,)), ((), ())), preferred_element_type=F32)


def roll64(v):
    return pltpu.roll(v, 64, 1)


def low_lanes(rows):
    return lax.broadcasted_iota(jnp.int32, (rows, 128), 1) < 64


def normalize(v):
    mean = jnp.mean(v, axis=-1, keepdims=True)
    cen = v - mean
    inv = lax.rsqrt(jnp.mean(cen * cen, axis=-1, keepdims=True) + EPS)
    return cen * inv, inv


def norm_back(u, hat, inv):
    m0 = jnp.mean(u, axis=-1, keepdims=True)
    m1 = jnp.mean(u * hat, axis=-1, keepdims=True)
    return inv * (u - m0 - hat * m1)


def chain_len(d, b):
    return 4 if d == b else 3


def slot(d, b, s):
    return d * 8 + b * 4 + s


def kernel(
    act_h, cot_h, gain_h, win_h, wout_h, qg_h, kg_h,
    gx_ref, gwi_ref, gwo_ref, gs_ref,
    act_v, cot_v, gain_v, wout, qg_v, kg_v,
    wf, xg, xs, xn, xt, xts, dy2, ot, jt, gp2,
    in_snd, in_rcv, out_snd, out_rcv, dxt, dxr, ps, ga, gb,
    ld, w_s, w_r, wc_s, wc_r, x_s, x_r, sb_s, sb_r,
    i_s, i_r, o_s, o_r, a_s, a_r, ac_s, ac_r, d_s, d_r, p_s, p_r, g_s, g_r,
):
    dp = lax.axis_index("dp")
    mp = lax.axis_index("mp")
    y, h, c = dp // 4, (dp // 2) % 2, dp % 2
    l, z = mp // RING, mp % RING

    def wrap(i):
        return lax.rem(i + 2 * RING, RING)

    def dpi(yy, hh, cc):
        return (wrap(yy) * 2 + hh) * 2 + cc

    def mpi(ll, zz):
        return ll * RING + wrap(zz)

    def on_dp(yy, hh, cc):
        return {"dp": dpi(yy, hh, cc), "mp": mp}

    def on_mp(ll, zz):
        return {"dp": dp, "mp": mpi(ll, zz)}

    sibling = on_dp(y, h, 1 - c)
    even = z % 2

    loads = []
    for i, (src, dst) in enumerate(
        ((act_h, act_v), (cot_h, cot_v), (gain_h, gain_v), (win_h, wf.at[dp]), (qg_h, qg_v), (kg_h, kg_v), (wout_h, wout))
    ):
        cp = pltpu.make_async_copy(src, dst, ld.at[i])
        cp.start()
        loads.append(cp)

    barrier = pltpu.get_barrier_semaphore()
    peers = [on_dp(y + k, h, c) for k in range(1, RING)]
    peers += [sibling, on_dp(y, 1 - h, c), on_dp(y, 1 - h, 1 - c), on_dp(y + 1, 1 - h, c), on_dp(y - 1, 1 - h, c)]
    peers += [on_mp(l, z + k) for k in range(1, RING)] + [on_mp(1 - l, z + k) for k in range(RING)]
    for p in peers:
        pl.semaphore_signal(barrier, inc=1, device_id=p, device_id_type=pl.DeviceIdType.MESH)

    def natural_to_packed(n0, n1, rows):
        lo = low_lanes(rows)
        ev = jnp.full((rows, 128), even, jnp.int32) == 0
        r0, r1 = roll64(n0), roll64(n1)
        return jnp.where(ev, n0, jnp.where(lo, r0, r1)), jnp.where(ev, n1, r0)

    lo64 = low_lanes(64)
    ev64 = jnp.full((64, 128), even, jnp.int32) == 0
    first64 = lo64 == ev64
    lo128 = low_lanes(128)
    valid128 = lo128 == (jnp.full((128, 128), even, jnp.int32) == 0)

    for i in range(3):
        loads[i].wait()
    for src, base in ((act_v, 0), (cot_v, 192)):
        n0 = src[:, 0:128].astype(F32)
        t = src[:, 128:192].astype(F32)
        n1 = jnp.concatenate([t, t], axis=1)
        full, half = natural_to_packed(n0, n1, 128)
        xg[mp, base : base + 128, :] = full.astype(BF16)
        xg[mp, base + 128 : base + 192, :] = jnp.where(first64, half[0:64], roll64(half[64:128])).astype(BF16)
    t = jnp.broadcast_to(gain_v[:, 128:192], (8, 64))
    gain_full, gain_half = natural_to_packed(
        jnp.broadcast_to(gain_v[:, 0:128], (8, 128)), jnp.concatenate([t, t], axis=1), 8
    )
    xg[mp, 384:400, :] = jnp.concatenate([gain_full, gain_half], axis=0).astype(BF16)
    loads[3].wait()
    pl.semaphore_wait(barrier, len(peers))

    pending = []

    def remote(src, dst, snd, rcv, to):
        return pltpu.make_async_remote_copy(
            src_ref=src, dst_ref=dst, send_sem=snd, recv_sem=rcv, device_id=to, device_id_type=pl.DeviceIdType.MESH
        )

    def send(src, dst, snd, rcv, to):
        cp = remote(src, dst, snd, rcv, to)
        cp.start()
        pending.append(cp)

    class Gather:
        def __init__(self, blk, snd, rcv, up, down, up_x, down_x, pair, forward=None):
            self.blk, self.snd, self.rcv = blk, snd, rcv
            self.to = ((up, up_x), (down, down_x))
            self.near = (up, down)
            self.pair, self.forward = pair, forward
            self.n_fwd = 0

        def _fwd(self, off, b):
            if self.forward is not None:
                s, r = self.forward
                ref = self.blk(off, b)
                send(ref, ref, s.at[self.n_fwd], r.at[self.n_fwd], sibling)
                self.n_fwd += 1

        def start(self):
            own = self.blk(0, 0)
            for b in range(2):
                for d in range(2):
                    i = slot(d, b, 0)
                    send(own, own, self.snd.at[i], self.rcv.at[i], self.to[d][b])
                if b == 0:
                    send(own, own, self.snd.at[16], self.rcv.at[16], self.pair)
            self._fwd(0, 0)

        def arrive(self, off, b, i, to):
            ref = self.blk(off, b)
            remote(ref, ref, self.snd.at[i], self.rcv.at[i], to).wait_recv()

        def step(self, st):
            for b in range(2):
                for d in range(2):
                    if st == 4 and d != b:
                        continue
                    off = -st if d == 0 else st
                    self.arrive(off, b, slot(d, b, st - 1), self.near[d])
                    if st < 3 or (st == 3 and d == b):
                        i = slot(d, b, st)
                        ref = self.blk(off, b)
                        send(ref, ref, self.snd.at[i], self.rcv.at[i], self.near[d])
                    self._fwd(off, b)
            if st == 1:
                self.arrive(0, 1, 16, self.pair)
                self._fwd(0, 1)

    def half_h(b):
        return h if b == 0 else 1 - h

    def half_l(b):
        return l if b == 0 else 1 - l

    y_near = (on_dp(y + 1, h, c), on_dp(y - 1, h, c), on_dp(y + 1, 1 - h, c), on_dp(y - 1, 1 - h, c), on_dp(y, 1 - h, c))
    z_near = (on_mp(l, z + 1), on_mp(l, z - 1), on_mp(1 - l, z + 1), on_mp(1 - l, z - 1), on_mp(1 - l, z))
    gx_ring = Gather(lambda off, b: xg.at[mpi(half_l(b), z + off)], x_s, x_r, *z_near)
    gw_ring = Gather(lambda off, b: wf.at[dpi(y + off, half_h(b), c)], w_s, w_r, *y_near, forward=(wc_s, wc_r))

    gx_ring.start()
    gw_ring.start()

    for i in range(4, 7):
        loads[i].wait()

    def unpack(j, base):
        ea, eb = 2 * j, 2 * j + 1
        a = xg[ea, base + 128 : base + 192, :].astype(F32)
        b = xg[eb, base + 128 : base + 192, :].astype(F32)
        mid = jnp.concatenate([jnp.where(lo64, a, b), roll64(jnp.where(lo64, b, a))], axis=0)
        return (xg[ea, base : base + 128, :], mid, xg[eb, base : base + 128, :])

    def process(q, carry):
        gcat, sums = carry
        for b in range(2):
            j = half_l(b) * 4 + lax.rem(z // 2 + q + 4, 4)
            x0, xm, x2 = unpack(j, 0)
            x0, x2 = x0.astype(F32), x2.astype(F32)
            xs[j, :, 0:128] = x0
            xs[j, :, 128:256] = xm
            xs[j, :, 256:384] = x2
            sums = sums + (x0 + xm + x2)
            d0, dm, d2 = unpack(j, 192)
            dy = jnp.concatenate([d0, dm.astype(BF16), d2], axis=1)
            dy2[j, 0:128, :] = dy
            gcat = gcat + dot_t(dy, wout[:, pl.ds(pl.multiple_of(j * 384, 128), 384)])
        return gcat, sums

    carry = (jnp.zeros((128, 256), F32), jnp.zeros((128, 128), F32))
    for st in range(1, 5):
        gx_ring.step(st)
        gw_ring.step(st)
        if st == 1:
            carry = process(0, carry)
        if st == 3:
            carry = process(1, carry)
            carry = process(-1, carry)
        if st == 4:
            carry = process(2, carry)
    grad_cat, sums = carry
    send(dy2.at[:, 0:128], dy2.at[:, 128:256], sb_s.at[0], sb_r.at[0], sibling)

    x_mean = jnp.sum(sums, axis=-1, keepdims=True) * (1.0 / WIDTH)

    def var_body(j, acc):
        v = xs[j] - x_mean
        v = v * v
        return acc + (v[:, 0:128] + v[:, 128:256] + v[:, 256:384])

    var = lax.fori_loop(0, 8, var_body, jnp.zeros((128, 128), F32))
    x_inv = lax.rsqrt(jnp.sum(var, axis=-1, keepdims=True) * (1.0 / WIDTH) + EPS)

    for i in range(16):
        ref = wf.at[0]
        remote(ref, ref, wc_s.at[i], wc_r.at[i], sibling).wait_recv()

    def proj_body(j, acc):
        ga_ = xg[2 * j, 384:400, :].astype(F32)
        gb_ = xg[2 * j + 1, 384:400, :].astype(F32)
        gm = jnp.where(low_lanes(1), ga_[8:9], gb_[8:9])
        gain = jnp.concatenate([ga_[0:1], gm, gb_[0:1]], axis=1)
        v = (xs[j] - x_mean) * x_inv * gain
        vb = v.astype(BF16)
        xn[j] = vb
        w = wf[pl.ds(4 * j, 4)].reshape(384, 512)
        return acc + dot(vb, w)

    proj = lax.fori_loop(0, 8, proj_body, jnp.zeros((128, 512), F32))

    pre = proj[:, 384:512]
    cdf = 0.5 * (1.0 + lax.erf(pre * 0.7071067811865476))
    pdf = jnp.exp(-0.5 * pre * pre) * 0.3989422804014327
    act = pre * cdf
    grad_pre = grad_cat[:, 128:256] * (cdf + pre * pdf)

    scaling = 128.0 ** -0.5
    qg, kg = qg_v[...].astype(F32), kg_v[...].astype(F32)
    q_hat, q_inv = normalize(proj[:, 0:128])
    k_hat, k_inv = normalize(proj[:, 128:256])
    qn, kn = (q_hat * qg).astype(BF16), (k_hat * kg).astype(BF16)
    v_bf = proj[:, 256:384].astype(BF16)
    go = grad_cat[:, 0:128].astype(BF16)
    sc = dot_t(qn, kn) * scaling
    e = jnp.exp(sc - jnp.max(sc, axis=-1, keepdims=True))
    prob = e / jnp.sum(e, axis=-1, keepdims=True)
    out = dot(prob.astype(BF16), v_bf)

    is0 = jnp.full((128, 128), c, jnp.int32) == 0
    jt[0] = jnp.where(is0, out, act).T.astype(BF16)
    jt[1] = jnp.where(is0, act, out).T.astype(BF16)
    send(jt.at[1], jt.at[2], sb_s.at[1], sb_r.at[1], sibling)

    gprob = dot_t(go, v_bf)
    grad_v = dot(prob.T.astype(BF16), go)
    gsc = prob * (gprob - jnp.sum(prob * gprob, axis=-1, keepdims=True)) * scaling
    gqn = dot(gsc.astype(BF16), kn)
    gkn = dot(gsc.T.astype(BF16), qn)
    gqg = jnp.sum(gqn * q_hat, axis=0, keepdims=True)
    gkg = jnp.sum(gkn * k_hat, axis=0, keepdims=True)
    grad_q = norm_back(gqn * qg, q_hat, q_inv)
    grad_k = norm_back(gkn * kg, k_hat, k_inv)
    gp = jnp.concatenate([grad_q, grad_k, grad_v, grad_pre], axis=1).astype(BF16)
    gp2[0] = gp
    send(gp2.at[0], gp2.at[1], sb_s.at[2], sb_r.at[2], sibling)

    def xt_body(j, _):
        t = xn[j].astype(F32)
        t = jnp.concatenate([t[:, k * 128 : (k + 1) * 128].T for k in range(3)], axis=0).astype(BF16)
        xt[pl.ds(2 * j, 2)] = t.reshape(2, 2, 96, 128)
        return 0

    lax.fori_loop(0, 8, xt_body, 0)
    send(xt.at[:, 1 - c], xts, sb_s.at[3], sb_r.at[3], sibling)

    def dx_body(j, _):
        w = wf[pl.ds(4 * j, 4)].reshape(384, 512)
        t = dot_t(gp2[0], w)
        mid = t[:, 128:256]
        top, bottom = mid[0:64], roll64(mid[64:128])
        dxt[2 * j, 0:128, :] = t[:, 0:128].astype(BF16)
        dxt[2 * j, 128:192, :] = jnp.where(lo64, top, bottom).astype(BF16)
        dxt[2 * j + 1, 0:128, :] = t[:, 256:384].astype(BF16)
        dxt[2 * j + 1, 128:192, :] = jnp.where(lo64, bottom, top).astype(BF16)
        return 0

    lax.fori_loop(0, 8, dx_body, 0)
    mp_peers = [(b, k) for k in (4, 3, 5, 2, 6, 1, 7, 0) for b in range(2) if (b, k) != (0, 0)]
    for b, k in mp_peers:
        i = b * 8 + k
        send(dxt.at[mpi(half_l(b), z + k)], dxr.at[i], d_s.at[i], d_r.at[i], on_mp(half_l(b), z + k))

    remote(jt.at[1], jt.at[2], sb_s.at[1], sb_r.at[1], sibling).wait_recv()
    remote(dy2.at[:, 0:128], dy2.at[:, 128:256], sb_s.at[0], sb_r.at[0], sibling).wait_recv()
    jt_cat = jnp.concatenate([jt[0], jt[2]], axis=1)

    def ot_body(j, _):
        t = dot(jt_cat, dy2[j])
        ot[pl.ds(2 * j, 2)] = t.reshape(2, 64, 384)
        return 0

    lax.fori_loop(0, 8, ot_body, 0)

    class Reduce:
        def __init__(self, term, snd, rcv, s, r, near, pair):
            self.term, self.snd, self.rcv, self.s, self.r = term, snd, rcv, s, r
            self.near, self.pair = near, pair

        def _send(self, i, value, to):
            self.snd[i] = value.astype(BF16)
            send(self.snd.at[i], self.rcv.at[i], self.s.at[i], self.r.at[i], to)

        def _arrived(self, i, to):
            remote(self.snd.at[i], self.rcv.at[i], self.s.at[i], self.r.at[i], to).wait_recv()
            return self.rcv[i].astype(F32)

        def step(self, st):
            for b in range(2):
                for d in range(2):
                    n = chain_len(d, b)
                    if st >= n:
                        continue
                    off = (n - st) if d == 0 else st - n
                    value = self.term(off, b)
                    if st > 0:
                        value = value + self._arrived(slot(d, b, st - 1), self.near[d])
                    self._send(slot(d, b, st), value, self.near[d])

        def total(self, b):
            value = self.term(0, b)
            for d in range(2):
                value = value + self._arrived(slot(d, b, chain_len(d, b) - 1), self.near[d])
            return value

        def finish(self):
            self._send(7, self.total(1), self.pair)
            return self.total(0)

        def partner(self):
            return self._arrived(7, self.pair)

    def term_out(off, b):
        return ot[wrap(y + off) * 2 + half_h(b)]

    def term_in(off, b):
        i = wrap(y + off) * 2 + half_h(b)
        return dot(jnp.concatenate([xt[i, c], xts[i]], axis=1), gp2[...].reshape(256, 512))

    ring_out = Reduce(term_out, out_snd, out_rcv, o_s, o_r, y_near[0:2], y_near[4])
    ring_in = Reduce(term_in, in_snd, in_rcv, i_s, i_r, y_near[0:2], y_near[4])

    ring_out.step(0)
    remote(gp2.at[0], gp2.at[1], sb_s.at[2], sb_r.at[2], sibling).wait_recv()
    remote(xt.at[:, 1 - c], xts, sb_s.at[3], sb_r.at[3], sibling).wait_recv()
    ring_in.step(0)
    for st in range(1, 4):
        ring_out.step(st)
        ring_in.step(st)
    out_sum = ring_out.finish()

    dxn = dxt[mp].astype(F32)
    for b, k in mp_peers:
        i = b * 8 + k
        remote(dxt.at[0], dxr.at[i], d_s.at[i], d_r.at[i], on_mp(half_l(b), z + k)).wait_recv()
        dxn = dxn + dxr[i].astype(F32)

    def tiles(packed):
        half = packed[128:192]
        return packed[0:128], jnp.where(valid128, jnp.concatenate([half, roll64(half)], axis=0), 0.0)

    own = xg[mp].astype(F32)
    x_full, x_half = tiles(own[0:192])
    dx_full, dx_half = tiles(dxn)
    hat_full = (x_full - x_mean) * x_inv
    hat_half = jnp.where(valid128, (x_half - x_mean) * x_inv, 0.0)
    ln_full = jnp.sum(dx_full * hat_full, axis=0, keepdims=True)
    ln_half = jnp.sum(dx_half * hat_half, axis=0, keepdims=True)
    s_full, s_half = dx_full * own[384:385], dx_half * jnp.where(low_lanes(1) == (jnp.full((1, 128), even, jnp.int32) == 0), own[392:393], 0.0)
    sum0 = jnp.sum(s_full + s_half, axis=-1, keepdims=True)
    sum1 = jnp.sum(s_full * hat_full + s_half * hat_half, axis=-1, keepdims=True)
    lane128 = lax.broadcasted_iota(jnp.int32, (128, 128), 1)
    cols = jnp.where(lane128 == 0, sum0, jnp.where(lane128 == 1, sum1, 0.0))
    ps[0] = cols.T[0:8]
    for b, k in mp_peers:
        i = b * 8 + k
        send(ps.at[0], ps.at[i], p_s.at[i], p_r.at[i], on_mp(half_l(b), z + k))

    ga[0] = jnp.concatenate([gqg, gkg, ln_full, ln_half, jnp.zeros((4, 128), F32)], axis=0)
    quad = (on_dp(y, h, 1 - c), on_dp(y, 1 - h, c), on_dp(y, 1 - h, 1 - c))
    for i, p in enumerate(quad):
        send(ga.at[0], ga.at[i + 1], g_s.at[i], g_r.at[i], p)

    def blk_out(off, b):
        return gwo_ref.at[dpi(y + off, half_h(b), c)]

    gwo_ref[dp] = ((out_sum + ring_out.partner()) * FACTOR).astype(BF16)
    ga_ring = Gather(blk_out, a_s, a_r, *y_near, forward=(ac_s, ac_r))
    ga_ring.start()

    in_sum = ring_in.finish()

    for i, p in enumerate(quad):
        remote(ga.at[0], ga.at[i + 1], g_s.at[i], g_r.at[i], p).wait_recv()
    gb[0] = (ga[0] + ga[1]) + (ga[2] + ga[3])
    for k in range(1, RING):
        send(gb.at[0], gb.at[k], g_s.at[2 + k], g_r.at[2 + k], on_dp(y + k, h, c))

    ga_ring.step(1)

    acc = ps[0]
    for b, k in mp_peers:
        i = b * 8 + k
        remote(ps.at[0], ps.at[i], p_s.at[i], p_r.at[i], on_mp(half_l(b), z + k)).wait_recv()
        acc = acc + ps[i]
    back = (jnp.concatenate([acc, jnp.zeros((120, 128), F32)], axis=0) * (1.0 / WIDTH)).T
    mean0, mean1 = back[:, 0:1], back[:, 1:2]
    c_full, c_half = tiles(own[192:384])
    r_full = c_full + x_inv * (s_full - mean0 - hat_full * mean1)
    r_half = c_half + x_inv * (s_half - mean0 - hat_half * mean1)

    def packed_to_natural(full, half, rows):
        ev = jnp.full((rows, 128), even, jnp.int32) == 0
        rf = roll64(full)
        return jnp.where(ev, full, jnp.where(low_lanes(rows), roll64(half), rf)), jnp.where(ev, half, rf)

    o0, o1 = packed_to_natural(r_full, r_half, 128)
    gx_ref[:, 0:128] = o0.astype(BF16)
    gx_ref[:, 128:192] = o1[:, 0:64].astype(BF16)

    ga_ring.step(2)
    gwi_ref[...] = ((in_sum + ring_in.partner()) * FACTOR).astype(BF16)
    ga_ring.step(3)
    total = gb[0]
    for k in range(1, RING):
        remote(gb.at[0], gb.at[k], g_s.at[2 + k], g_r.at[2 + k], on_dp(y + k, h, c)).wait_recv()
        total = total + gb[k]
    total = total * FACTOR
    g0, g1 = packed_to_natural(
        jnp.broadcast_to(total[2:3], (8, 128)), jnp.broadcast_to(total[3:4], (8, 128)), 8
    )
    gs_ref[...] = jnp.concatenate([total[0:2], g0[0:1], g1[0:1], jnp.zeros((4, 128), F32)], axis=0)
    ga_ring.step(4)
    for i in range(16):
        ref = gwo_ref.at[0]
        remote(ref, ref, ac_s.at[i], ac_r.at[i], sibling).wait_recv()
    for cp in pending:
        cp.wait_send()


def per_device(activations, cotangent, ln_gain, w_in, w_out, q_gain, k_gain):
    any_space = pl.BlockSpec(memory_space=pl.ANY)
    vmem = pl.BlockSpec(memory_space=pltpu.VMEM)
    dma = pltpu.SemaphoreType.DMA

    def buf(*shape, dtype=BF16):
        return pltpu.VMEM(shape, dtype)

    scratch = [
        buf(128, 192), buf(128, 192), buf(1, 192, dtype=F32), buf(256, 3072), buf(1, 128), buf(1, 128),
        buf(32, 96, 512),
        buf(16, 400, 128),
        buf(8, 128, 384, dtype=F32),
        buf(8, 128, 384),
        buf(16, 2, 96, 128), buf(16, 96, 128),
        buf(8, 256, 384),
        buf(16, 64, 384, dtype=F32),
        buf(3, 128, 128),
        buf(2, 128, 512),
        buf(16, 96, 512), buf(16, 96, 512), buf(16, 64, 384), buf(16, 64, 384),
        buf(16, 192, 128), buf(16, 192, 128),
        buf(16, 8, 128, dtype=F32), buf(4, 8, 128, dtype=F32), buf(8, 8, 128, dtype=F32),
        dma((7,)), dma((17,)), dma((17,)), dma((16,)), dma((16,)), dma((17,)), dma((17,)), dma((4,)), dma((4,)),
        dma((16,)), dma((16,)), dma((16,)), dma((16,)), dma((17,)), dma((17,)), dma((16,)), dma((16,)),
        dma((16,)), dma((16,)), dma((16,)), dma((16,)), dma((10,)), dma((10,)),
    ]
    grad_x, grad_w_in, grad_w_out, sums = pl.pallas_call(
        kernel,
        out_shape=(
            jax.ShapeDtypeStruct((128, 192), BF16),
            jax.ShapeDtypeStruct((96, 512), BF16),
            jax.ShapeDtypeStruct((32, 64, 384), BF16),
            jax.ShapeDtypeStruct((8, 128), F32),
        ),
        in_specs=[any_space] * 7,
        out_specs=(vmem,) * 4,
        scratch_shapes=scratch,
        compiler_params=pltpu.CompilerParams(collective_id=0, has_side_effects=True, vmem_limit_bytes=48 << 20),
    )(activations, cotangent, ln_gain.astype(F32).reshape(1, 192), w_in, w_out, q_gain, k_gain)
    grad_w_out = grad_w_out.reshape(8, 2, 2, 64, 384).transpose(2, 1, 3, 0, 4).reshape(256, 3072)
    grad_ln = jnp.concatenate([sums[2], sums[3, 0:64]])
    return grad_x, grad_w_in, grad_w_out, grad_ln, sums[0:1], sums[1:2]


def solution(mesh):
    in_specs = (P("dp", "mp"), P("dp", "mp"), P("mp"), P("dp", "mp"), P("mp", None), P("mp", None), P("mp", None))
    out_specs = (P("dp", "mp"), P("dp", "mp"), P("mp", None), P("mp"), P("mp", None), P("mp", None))
    return jax.shard_map(per_device, mesh=mesh, in_specs=in_specs, out_specs=out_specs, check_vma=False)
```

time: 626 us -> 112 us (0.18)
  waiting for transfers between devices: 375 us -> 0 us
  blocking collectives: 200 us -> 0 us
  Pallas kernels: 0 us -> 98.6 us
  matrix products: 16 us -> 0 us
  between operations: 14.8 us -> 0.67 us
  other arithmetic: 12.8 us -> 1.23 us
  local copies, waits for them, and re-layouts: 2.86 us -> 9.65 us
    reduce_scatter x2 -> x0, waiting for transfers between devices: 195 us -> none  [the longest x1 127 us: per_device(): lax.psum_scatter(lax.dot_general(x_normed, grad_proj, (((0,), (0,)), ((),...]
    psum x1 -> x0, waiting for transfers between devices: 175 us -> none  [per_device(): out_sum = lax.psum(out_term.astype(jnp.bfloat16), 'dp').astype(jnp.float32)]
    psum x2 -> x0, blocking collectives: 108 us -> none  [the longest x1 82.1 us: per_device(): ln_sum, q_sum, k_sum = lax.psum((ln_term, q_gain_grad, k_gain_grad), 'dp')]
    pallas_call x0 -> x1, Pallas kernels: none -> 98.6 us  [per_device(): pl.pallas_call(kernel, out_shape=(jax.ShapeDtypeStruct((128, 192), BF16),...]
    all_gather x2 -> x0, blocking collectives: 57 us -> none  [the longest x1 29.2 us: per_device(): dy_full = lax.all_gather(cotangent, 'mp', axis=1, tiled=True)]
    unnamed x1 -> x0, blocking collectives: 34.8 us -> none
    dot_general x11 -> x0, matrix products: 16 us -> none  [the longest x1 3.33 us: per_device(): projected = jnp.dot(x_normed, w_full, preferred_element_type=jnp.float32)]
    convert_element_type x7 -> x0, other arithmetic: 6.84 us -> none  [the longest x1 2.86 us: per_device(): (out_sum * factor).astype(jnp.bfloat16)]
  transfers between devices with their start and end apart: 4 -> 0, of which waited for: 4 -> 0; matrix products, arithmetic and copies ran while one was open for 3% -> 0% of each run, Pallas kernels for 0% -> 0%
where the time goes in v1:
time: 112 us; the launch traced here: 110 us
  Pallas kernels  98.6 us (88%)
  local copies, waits for them, and re-layouts  9.65 us (9%)
  other arithmetic  1.23 us (1%)
    pallas_call x1, Pallas kernels, per_device(): pl.pallas_call(kernel, out_shape=(jax.ShapeDtypeStruct((128, 192), BF16),...  98.6 us
    unnamed x13, local copies, waits for them, and re-layouts  8.2 us

profile of v1, /device:TPU:1, one launch (start us, length us, event | category | flops | bytes accessed | tf_op | source)
XLA Modules:
  0.0 110.2 jit_solution(15214296786555498398)
XLA Ops:
  0.6 0.7 reshape.27
  1.3 0.9 copy.13.act_h
  2.2 0.9 copy.14.cot_h
  3.1 0.0 copy-start
  3.1 1.4 %copy-done = bf16[256,3072]{1,0:T(8,128)(2,1)S(1)} copy-done((bf16[256,3072]{1,0:T(8,128)(2,1)S(1)}, bf16[256,3072]{1,0:T(8,128)(2,1)}, u32[]{:S(2)}) %copy-start) | copy-done | bytes 1572888
  4.5 0.0 copy-start.1
  4.5 0.9 copy-done.1
  5.4 0.0 copy-start.2
  5.4 0.7 copy-done.2
  6.1 0.0 copy-start.3
  6.1 0.7 copy-done.3
  6.7 98.6 %shard_map.118 = (bf16[128,192]{1,0:T(8,128)(2,1)S(1)}, bf16[96,512]{1,0:T(8,128)(2,1)S(1)}, bf16[32,64,384]{2,1,0:T(8,128)(2,1)S(1)}, f32[8,128]{1,0:T(8,128)S(1)}) custom-call(bf16[128,192]{1,0:T(8,128)(2,1)S(1)} %copy.13.act_h, bf16[128,192]{1,0:T(8,128)(2,1)S(1)} %copy.14.cot_h, f32[1,192]{1,0:T(1,128)S(1)} %bitcast.12, bf16[96,512]{1,0:T(8,128)(2,1)S(1)} %copy-done.1, ...), custom_call_target="tpu_custom_call" | custom-call | tf_op jit(solution)/shard_map/pallas_call | solution.py:512
  105.3 0.7 copy.16
  106.1 0.5 fusion
  106.6 0.6 pad_maximum_fusion
  107.2 0.9 copy.15
  108.1 1.4 %copy.17 = bf16[32,8,8,384]{3,1,2,0:T(8,128)(2,1)} copy(bf16[32,8,8,384]{3,2,1,0:T(8,128)(2,1)S(1)} %bitcast.13) | data formatting | bytes 3145728
  109.5 0.6 copy.19
  (1 shorter events, 0.0 us)
Async XLA Ops:
  3.1 1.4 %copy-start = (bf16[256,3072]{1,0:T(8,128)(2,1)S(1)}, bf16[256,3072]{1,0:T(8,128)(2,1)}, u32[]{:S(2)}) copy-start(bf16[256,3072]{1,0:T(8,128)(2,1)} %wout_h.1) | copy-start | bytes 4718596
  4.5 0.9 copy-start.1
  5.4 0.7 copy-start.2
  6.1 0.7 copy-start.3

commit v2 on v1

v2 whole, which is shorter than its diff:
```python
import jax
import jax.numpy as jnp
from jax import lax
from jax.experimental import pallas as pl
from jax.experimental.pallas import tpu as pltpu
from jax.sharding import PartitionSpec as P

F32 = jnp.float32
BF16 = jnp.bfloat16
EPS = 1e-6
RING = 8
WIDTH = 3072
FACTOR = 1.0 / 32.0


def dot(a, b):
    return jnp.dot(a, b, preferred_element_type=F32)


def dot_t(a, b):
    return lax.dot_general(a, b, (((1,), (1,)), ((), ())), preferred_element_type=F32)


def normalize(v):
    mean = jnp.mean(v, axis=-1, keepdims=True)
    cen = v - mean
    inv = lax.rsqrt(jnp.mean(cen * cen, axis=-1, keepdims=True) + EPS)
    return cen * inv, inv


def norm_back(u, hat, inv):
    m0 = jnp.mean(u, axis=-1, keepdims=True)
    m1 = jnp.mean(u * hat, axis=-1, keepdims=True)
    return inv * (u - m0 - hat * m1)


def rows8(v):
    return jnp.sum(v.reshape(v.shape[0] // 8, 8, 128), axis=0)


def row_of(column):
    return jnp.broadcast_to(column, (128, 128)).T[0:1]


def column_of(row):
    return jnp.broadcast_to(row, (128, 128)).T


def chain_len(d, b):
    return 4 if d == b else 3


def slot(d, b, s):
    return d * 8 + b * 4 + s


def kernel(
    act_h, cot_h, gain_h, win_h, wout_h, qg_h, kg_h,
    gx_ref, gwi_ref, gwo_ref, gs_ref,
    gain_v, wout, qg_v, kg_v,
    wf, xg, xt, xts, dys, ot, jt, gp2,
    in_snd, in_rcv, out_snd, out_rcv, dxt, dxr, ps, ga, gb,
    ld, w_s, w_r, wc_s, wc_r, x_s, x_r, sb_s, sb_r,
    i_s, i_r, o_s, o_r, a_s, a_r, ac_s, ac_r, d_s, d_r, p_s, p_r, g_s, g_r,
):
    dp = lax.axis_index("dp")
    mp = lax.axis_index("mp")
    y, h, c = dp // 4, (dp // 2) % 2, dp % 2
    l, z = mp // RING, mp % RING

    def wrap(i):
        return lax.rem(i + 2 * RING, RING)

    def dpi(yy, hh, cc):
        return (wrap(yy) * 2 + hh) * 2 + cc

    def mpi(ll, zz):
        return ll * RING + wrap(zz)

    def on_dp(yy, hh, cc):
        return {"dp": dpi(yy, hh, cc), "mp": mp}

    def on_mp(ll, zz):
        return {"dp": dp, "mp": mpi(ll, zz)}

    sibling = on_dp(y, h, 1 - c)

    loads = []
    for i, (src, dst) in enumerate(
        ((gain_h, gain_v), (act_h, xg.at[mp, 0:192]), (cot_h, xg.at[mp, 192:384]), (win_h, wf.at[dp]), (qg_h, qg_v), (kg_h, kg_v), (wout_h, wout))
    ):
        cp = pltpu.make_async_copy(src, dst, ld.at[i])
        cp.start()
        loads.append(cp)

    barrier = pltpu.get_barrier_semaphore()
    peers = [on_dp(y + k, h, c) for k in range(1, RING)]
    peers += [sibling, on_dp(y, 1 - h, c), on_dp(y, 1 - h, 1 - c), on_dp(y + 1, 1 - h, c), on_dp(y - 1, 1 - h, c)]
    peers += [on_mp(l, z + k) for k in range(1, RING)] + [on_mp(1 - l, z + k) for k in range(RING)]
    for p in peers:
        pl.semaphore_signal(barrier, inc=1, device_id=p, device_id_type=pl.DeviceIdType.MESH)

    loads[0].wait()
    gain = gain_v[...].astype(F32).reshape(1, 192)
    gain0 = gain[:, 0:128]
    gain1 = jnp.concatenate([gain[:, 128:192], gain[:, 128:192]], axis=1)
    xg[mp, 384:400, :] = jnp.concatenate(
        [jnp.broadcast_to(gain0, (8, 128)), jnp.broadcast_to(gain1, (8, 128))], axis=0
    ).astype(BF16)
    for i in range(1, 4):
        loads[i].wait()
    pl.semaphore_wait(barrier, len(peers))

    def remote(src, dst, snd, rcv, to):
        return pltpu.make_async_remote_copy(
            src_ref=src, dst_ref=dst, send_sem=snd, recv_sem=rcv, device_id=to, device_id_type=pl.DeviceIdType.MESH
        )

    def send(src, dst, snd, rcv, to):
        remote(src, dst, snd, rcv, to).start()

    def wait_bytes(ref, sem):
        pltpu.make_async_copy(ref, ref, sem).wait()

    class Gather:
        def __init__(self, blk, snd, rcv, near, forward=None):
            self.blk, self.snd, self.rcv = blk, snd, rcv
            self.near, self.pair, self.forward = near[0:2], near[2], forward

        def _fwd(self, off, b):
            if self.forward is not None:
                s, r = self.forward
                ref = self.blk(off, b)
                send(ref, ref, s, r, sibling)

        def _send(self, off, b, i, to):
            ref = self.blk(off, b)
            send(ref, ref, self.snd, self.rcv.at[i], to)

        def start(self):
            self._send(0, 0, 7, self.pair)
            for d in range(2):
                self._send(0, 0, slot(d, 0, 0), self.near[d])
            self._fwd(0, 0)

        def start_partner(self):
            self.arrive(0, 1, 7, self.pair)
            for d in range(2):
                self._send(0, 1, slot(d, 1, 0), self.near[d])
            self._fwd(0, 1)

        def arrive(self, off, b, i, to):
            ref = self.blk(off, b)
            remote(ref, ref, self.snd, self.rcv.at[i], to).wait_recv()

        def step(self, st, b):
            for d in range(2):
                n = chain_len(d, b)
                if st > n:
                    continue
                off = -st if d == 0 else st
                self.arrive(off, b, slot(d, b, st - 1), self.near[d])
                if st < n:
                    self._send(off, b, slot(d, b, st), self.near[d])
                self._fwd(off, b)

    def start_rings(rings):
        for r in rings:
            r.start()
        for r in rings:
            r.start_partner()

    def step_rings(rings, st):
        for b in range(2):
            for r in rings:
                r.step(st, b)

    def half_h(b):
        return h if b == 0 else 1 - h

    def half_l(b):
        return l if b == 0 else 1 - l

    y_near = (on_dp(y + 1, h, c), on_dp(y - 1, h, c), on_dp(y, 1 - h, c))
    z_near = (on_mp(l, z + 1), on_mp(l, z - 1), on_mp(1 - l, z))
    gx_ring = Gather(lambda off, b: xg.at[mpi(half_l(b), z + off)], x_s, x_r, z_near)
    gw_ring = Gather(lambda off, b: wf.at[dpi(y + off, half_h(b), c)], w_s, w_r, y_near, forward=(wc_s, wc_r))
    start_rings((gx_ring, gw_ring))

    for i in range(4, 7):
        loads[i].wait()

    def process(q, carry):
        gcat, sums = carry
        for b in range(2):
            j = half_l(b) * 4 + lax.rem(z // 2 + q + 4, 4)
            pair = xg[pl.ds(2 * j, 2)]
            sums = sums + rows8(pair[:, 0:192].reshape(384, 128).astype(F32))
            dy = pair[:, 192:384].reshape(384, 128)
            gcat = gcat + dot(wout[:, pl.ds(pl.multiple_of(j * 384, 128), 384)], dy)
        return gcat, sums

    carry = (jnp.zeros((256, 128), F32), jnp.zeros((8, 128), F32))
    for st in range(1, 5):
        step_rings((gx_ring, gw_ring), st)
        if st == 1:
            carry = process(0, carry)
        if st == 3:
            carry = process(1, carry)
            carry = process(-1, carry)
        if st == 4:
            carry = process(2, carry)
    grad_cat, sums = carry
    send(xg.at[:, 192:384], dys, sb_s.at[0], sb_r.at[0], sibling)

    x_mean = jnp.sum(sums, axis=0, keepdims=True) * (1.0 / WIDTH)

    def var_body(m, acc):
        v = xg[m, 0:192, :].astype(F32) - x_mean
        return acc + rows8(v * v)

    var = lax.fori_loop(0, 16, var_body, jnp.zeros((8, 128), F32))
    x_inv = lax.rsqrt(jnp.sum(var, axis=0, keepdims=True) * (1.0 / WIDTH) + EPS)

    gain_rows = []
    for m in range(16):
        t = xg[m, 384:400, :].astype(F32)
        gain_rows += [t[0:1], t[8:9]]
    gains = jnp.concatenate(gain_rows + [jnp.zeros((96, 128), F32)], axis=0).T

    wait_bytes(wf.at[0:16], wc_r)

    proj = jnp.zeros((128, 512), F32)
    for j in range(8):
        parts = []
        for m in (2 * j, 2 * j + 1):
            v = (xg[m, 0:192, :].astype(F32) - x_mean) * x_inv
            top = v[0:128] * gains[:, 2 * m : 2 * m + 1]
            bottom = v[128:192] * gains[0:64, 2 * m + 1 : 2 * m + 2]
            parts += [top, bottom]
        v = jnp.concatenate(parts, axis=0)
        xt[2 * j : 2 * j + 2] = v.astype(BF16).reshape(2, 2, 96, 128)
        vt = jnp.concatenate([v[k * 128 : (k + 1) * 128].T for k in range(3)], axis=1).astype(BF16)
        proj = proj + dot(vt, wf[4 * j : 4 * j + 4].reshape(384, 512))
    send(xt.at[:, 1 - c], xts, sb_s.at[3], sb_r.at[3], sibling)

    pre = proj[:, 384:512]
    cdf = 0.5 * (1.0 + lax.erf(pre * 0.7071067811865476))
    pdf = jnp.exp(-0.5 * pre * pre) * 0.3989422804014327
    act = pre * cdf
    grad_pre = grad_cat[128:256].T * (cdf + pre * pdf)

    scaling = 128.0 ** -0.5
    qg, kg = qg_v[...].astype(F32), kg_v[...].astype(F32)
    q_hat, q_inv = normalize(proj[:, 0:128])
    k_hat, k_inv = normalize(proj[:, 128:256])
    qn, kn = (q_hat * qg).astype(BF16), (k_hat * kg).astype(BF16)
    v_bf = proj[:, 256:384].astype(BF16)
    go = grad_cat[0:128].T.astype(BF16)
    sc = dot_t(qn, kn) * scaling
    e = jnp.exp(sc - jnp.max(sc, axis=-1, keepdims=True))
    prob = e / jnp.sum(e, axis=-1, keepdims=True)
    out = dot(prob.astype(BF16), v_bf)

    is0 = jnp.full((128, 128), c, jnp.int32) == 0
    jt[0] = jnp.where(is0, out, act).T.astype(BF16)
    jt[1] = jnp.where(is0, act, out).T.astype(BF16)
    send(jt.at[1], jt.at[2], sb_s.at[1], sb_r.at[1], sibling)

    gprob = dot_t(go, v_bf)
    grad_v = dot(prob.T.astype(BF16), go)
    gsc = prob * (gprob - jnp.sum(prob * gprob, axis=-1, keepdims=True)) * scaling
    gqn = dot(gsc.astype(BF16), kn)
    gkn = dot(gsc.T.astype(BF16), qn)
    gqg = jnp.sum(gqn * q_hat, axis=0, keepdims=True)
    gkg = jnp.sum(gkn * k_hat, axis=0, keepdims=True)
    grad_q = norm_back(gqn * qg, q_hat, q_inv)
    grad_k = norm_back(gkn * kg, k_hat, k_inv)
    gp = jnp.concatenate([grad_q, grad_k, grad_v, grad_pre], axis=1).astype(BF16)
    gp2[0] = gp
    send(gp2.at[0], gp2.at[1], sb_s.at[2], sb_r.at[2], sibling)

    def dx_body(j, _):
        w = wf[pl.ds(4 * j, 4)].reshape(384, 512)
        dxt[pl.ds(2 * j, 2)] = dot_t(w, gp2[0]).astype(BF16).reshape(2, 192, 128)
        return 0

    lax.fori_loop(0, 8, dx_body, 0)
    mp_peers = [(b, k) for k in (4, 3, 5, 2, 6, 1, 7, 0) for b in range(2) if (b, k) != (0, 0)]
    for b, k in mp_peers:
        i = b * 8 + k
        send(dxt.at[mpi(half_l(b), z + k)], dxr.at[i], d_s, d_r, on_mp(half_l(b), z + k))

    remote(jt.at[1], jt.at[2], sb_s.at[1], sb_r.at[1], sibling).wait_recv()
    remote(xg.at[:, 192:384], dys, sb_s.at[0], sb_r.at[0], sibling).wait_recv()
    jt_cat = jnp.concatenate([jt[0], jt[2]], axis=1)

    def ot_body(j, _):
        own = xg[pl.ds(2 * j, 2), 192:384, :].reshape(384, 128)
        other = dys[pl.ds(2 * j, 2)].reshape(384, 128)
        t = dot_t(jt_cat, jnp.concatenate([own, other], axis=1))
        ot[pl.ds(2 * j, 2)] = t.reshape(2, 64, 384)
        return 0

    lax.fori_loop(0, 8, ot_body, 0)

    class Reduce:
        def __init__(self, term, snd, rcv, s, r, near):
            self.term, self.snd, self.rcv, self.s, self.r = term, snd, rcv, s, r
            self.near, self.pair = near[0:2], near[2]

        def _send(self, i, value, to):
            self.snd[i] = value.astype(BF16)
            send(self.snd.at[i], self.rcv.at[i], self.s, self.r.at[i], to)

        def arrived(self, i, to):
            remote(self.snd.at[i], self.rcv.at[i], self.s, self.r.at[i], to).wait_recv()
            return self.rcv[i].astype(F32)

        def step(self, st):
            for b in range(2):
                for d in range(2):
                    n = chain_len(d, b)
                    if st >= n:
                        continue
                    off = (n - st) if d == 0 else st - n
                    value = self.term(off, b)
                    if st > 0:
                        value = value + self.arrived(slot(d, b, st - 1), self.near[d])
                    self._send(slot(d, b, st), value, self.near[d])

        def total(self, b):
            value = self.term(0, b)
            for d in range(2):
                value = value + self.arrived(slot(d, b, chain_len(d, b) - 1), self.near[d])
            return value

        def finish(self):
            self._send(7, self.total(1), self.pair)
            return self.total(0)

        def partner(self):
            return self.arrived(7, self.pair)

    def term_out(off, b):
        return ot[wrap(y + off) * 2 + half_h(b)]

    def term_in(off, b):
        i = wrap(y + off) * 2 + half_h(b)
        return dot(jnp.concatenate([xt[i, c], xts[i]], axis=1), gp2[...].reshape(256, 512))

    ring_out = Reduce(term_out, out_snd, out_rcv, o_s, o_r, y_near)
    ring_in = Reduce(term_in, in_snd, in_rcv, i_s, i_r, y_near)

    ring_out.step(0)
    remote(gp2.at[0], gp2.at[1], sb_s.at[2], sb_r.at[2], sibling).wait_recv()
    remote(xt.at[:, 1 - c], xts, sb_s.at[3], sb_r.at[3], sibling).wait_recv()
    ring_in.step(0)
    for st in range(1, 4):
        ring_out.step(st)
        ring_in.step(st)
    out_sum = ring_out.finish()

    dxn = dxt[mp].astype(F32)
    wait_bytes(dxr.at[1:16], d_r)
    for i in range(1, 16):
        dxn = dxn + dxr[i].astype(F32)

    own_gain = jnp.concatenate([column_of(gain0), column_of(gain1)[0:64]], axis=0)
    hat = (xg[mp, 0:192, :].astype(F32) - x_mean) * x_inv
    ln_column = jnp.sum(dxn * hat, axis=1, keepdims=True)
    scaled = dxn * own_gain
    sum0 = jnp.sum(scaled, axis=0, keepdims=True)
    sum1 = jnp.sum(scaled * hat, axis=0, keepdims=True)
    ps[0] = jnp.concatenate([sum0, sum1, jnp.zeros((6, 128), F32)], axis=0)
    for b, k in mp_peers:
        i = b * 8 + k
        send(ps.at[0], ps.at[i], p_s, p_r, on_mp(half_l(b), z + k))

    ln0 = row_of(ln_column[0:128])
    ln1 = row_of(jnp.concatenate([ln_column[128:192], jnp.zeros((64, 1), F32)], axis=0))
    ga[0] = jnp.concatenate([gqg, gkg, ln0, ln1, jnp.zeros((4, 128), F32)], axis=0)
    quad = (on_dp(y, h, 1 - c), on_dp(y, 1 - h, c), on_dp(y, 1 - h, 1 - c))
    for i, p in enumerate(quad):
        send(ga.at[0], ga.at[i + 1], g_s.at[0], g_r.at[0], p)

    def out_block(yy, hh):
        rows = pl.ds(pl.multiple_of(c * 128 + hh * 64, 64), 64)
        return gwo_ref.at[rows, pl.ds(pl.multiple_of(wrap(yy) * 384, 128), 384)]

    def blk_out(off, b):
        return out_block(y + off, half_h(b))

    out_block(y, h)[...] = ((out_sum + ring_out.partner()) * FACTOR).astype(BF16)
    ga_ring = Gather(blk_out, a_s, a_r, y_near, forward=(ac_s, ac_r))
    ga_ring.start()

    in_sum = ring_in.finish()
    ga_ring.start_partner()

    wait_bytes(ga.at[1:4], g_r.at[0])
    gb[0] = (ga[0] + ga[1]) + (ga[2] + ga[3])
    for k in range(1, RING):
        send(gb.at[0], gb.at[k], g_s.at[1], g_r.at[1], on_dp(y + k, h, c))

    step_rings((ga_ring,), 1)

    acc = ps[0]
    wait_bytes(ps.at[1:16], p_r)
    for i in range(1, 16):
        acc = acc + ps[i]
    mean0, mean1 = acc[0:1] * (1.0 / WIDTH), acc[1:2] * (1.0 / WIDTH)
    cot_own = xg[mp, 192:384, :].astype(F32)
    gx_ref[...] = (cot_own + x_inv * (scaled - mean0 - hat * mean1)).astype(BF16)

    step_rings((ga_ring,), 2)
    gwi_ref[...] = ((in_sum + ring_in.partner()) * FACTOR).astype(BF16)
    step_rings((ga_ring,), 3)
    total = gb[0]
    wait_bytes(gb.at[1:8], g_r.at[1])
    for k in range(1, RING):
        total = total + gb[k]
    gs_ref[...] = total * FACTOR
    step_rings((ga_ring,), 4)
    wait_bytes(out_snd.at[0:16], ac_r)

    for ref, sem in (
        (xg.at[0:15], x_s), (wf.at[0:15], w_s), (wf.at[0:16], wc_s),
        (dys, sb_s.at[0]), (jt.at[1], sb_s.at[1]), (gp2.at[0], sb_s.at[2]), (xts, sb_s.at[3]),
        (in_snd.at[0:15], i_s), (out_snd.at[0:15], o_s), (out_snd.at[0:15], a_s), (out_snd.at[0:16], ac_s),
        (dxt.at[0:15], d_s), (ps.at[0:15], p_s), (ga.at[0:3], g_s.at[0]), (gb.at[0:7], g_s.at[1]),
    ):
        wait_bytes(ref, sem)


def per_device(activations, cotangent, ln_gain, w_in, w_out, q_gain, k_gain):
    hbm = pl.BlockSpec(memory_space=pltpu.HBM)
    vmem = pl.BlockSpec(memory_space=pltpu.VMEM)
    dma = pltpu.SemaphoreType.DMA

    def buf(*shape, dtype=BF16):
        return pltpu.VMEM(shape, dtype)

    scratch = [
        buf(192), buf(256, 3072), buf(1, 128), buf(1, 128),
        buf(32, 96, 512),
        buf(16, 400, 128),
        buf(16, 2, 96, 128), buf(16, 96, 128),
        buf(16, 192, 128),
        buf(16, 64, 384, dtype=F32),
        buf(3, 128, 128),
        buf(2, 128, 512),
        buf(16, 96, 512), buf(16, 96, 512), buf(16, 64, 384), buf(16, 64, 384),
        buf(16, 192, 128), buf(16, 192, 128),
        buf(16, 8, 128, dtype=F32), buf(4, 8, 128, dtype=F32), buf(8, 8, 128, dtype=F32),
        dma((7,)), dma, dma((16,)), dma, dma, dma, dma((16,)), dma((4,)), dma((4,)),
        dma, dma((16,)), dma, dma((16,)), dma, dma((16,)), dma, dma,
        dma, dma, dma, dma, dma((2,)), dma((2,)),
    ]
    args = (activations.T, cotangent.T, ln_gain, w_in, w_out, q_gain, k_gain)
    grad_x, grad_w_in, grad_w_out, sums = pl.pallas_call(
        kernel,
        out_shape=(
            jax.ShapeDtypeStruct((192, 128), BF16),
            jax.ShapeDtypeStruct((96, 512), BF16),
            jax.ShapeDtypeStruct((256, 3072), BF16),
            jax.ShapeDtypeStruct((8, 128), F32),
        ),
        in_specs=[hbm] * 7,
        out_specs=(vmem,) * 4,
        scratch_shapes=scratch,
        compiler_params=pltpu.CompilerParams(collective_id=0, has_side_effects=True, vmem_limit_bytes=48 << 20),
    )(*(pltpu.with_memory_space_constraint(a, pltpu.HBM) for a in args))
    grad_ln = jnp.concatenate([sums[2], sums[3, 0:64]])
    return grad_x.T, grad_w_in, grad_w_out, grad_ln, sums[0:1], sums[1:2]


def solution(mesh):
    in_specs = (P("dp", "mp"), P("dp", "mp"), P("mp"), P("dp", "mp"), P("mp", None), P("mp", None), P("mp", None))
    out_specs = (P("dp", "mp"), P("dp", "mp"), P("mp", None), P("mp"), P("mp", None), P("mp", None))
    return jax.shard_map(per_device, mesh=mesh, in_specs=in_specs, out_specs=out_specs, check_vma=False)
```

time: 112 us -> 96.6 us (0.86); the launches traced: 110 us -> 96.5 us
  local copies, waits for them, and re-layouts: 9.65 us -> 2.92 us
  Pallas kernels: 98.6 us -> 92.4 us
    pallas_call x1, Pallas kernels: 98.6 us -> 92.4 us  [per_device(): pl.pallas_call(kernel, out_shape=(jax.ShapeDtypeStruct((192, 128), BF16),...]
    unnamed x13 -> x3, local copies, waits for them, and re-layouts: 8.2 us -> 2.4 us
where the time goes in v2:
time: 96.6 us; the launch traced here: 96.5 us
  Pallas kernels  92.4 us (96%)
  local copies, waits for them, and re-layouts  2.92 us (3%)
    pallas_call x1, Pallas kernels, per_device(): pl.pallas_call(kernel, out_shape=(jax.ShapeDtypeStruct((192, 128), BF16),...  92.4 us
    unnamed x3, local copies, waits for them, and re-layouts  2.4 us

profile of v2, /device:TPU:1, one launch (start us, length us, event | category | flops | bytes accessed | tf_op | source)
XLA Modules:
  0.0 96.5 jit_solution(5211289722899283323)
XLA Ops:
  0.6 92.4 %shard_map.118 = (bf16[192,128]{1,0:T(8,128)(2,1)S(1)}, bf16[96,512]{1,0:T(8,128)(2,1)S(1)}, bf16[256,3072]{1,0:T(8,128)(2,1)S(1)}, f32[8,128]{1,0:T(8,128)S(1)}) custom-call(bf16[192,128]{1,0:T(8,128)(2,1)} %bitcast.8, bf16[192,128]{1,0:T(8,128)(2,1)} %bitcast.9, bf16[192]{0:T(256)(128)(2,1)} %gain_h.1, bf16[96,512]{1,0:T(8,128)(2,1)} %win_h.1, ...), custom_call_target="tpu_custom_call" | custom-call | tf_op jit(solution)/shard_map/pallas_call | solution.py:461
  93.0 0.5 fusion
  93.5 0.6 pad_maximum_fusion
  94.1 0.6 copy.16
  94.7 0.6 copy.17
  95.4 1.1 %copy.18 = bf16[256,3072]{1,0:T(8,128)(2,1)} copy(bf16[256,3072]{1,0:T(8,128)(2,1)S(1)} %get-tuple-element.25) | data formatting | bytes 3145728
  (1 shorter events, 0.0 us)

commit v3 on v2

--- a/solution.py
+++ b/solution.py
@@ -59,9 +59,9 @@
     gx_ref, gwi_ref, gwo_ref, gs_ref,
     gain_v, wout, qg_v, kg_v,
     wf, xg, xt, xts, dys, ot, jt, gp2,
-    in_snd, in_rcv, out_snd, out_rcv, dxt, dxr, ps, ga, gb,
+    in_snd, in_rcv, out_x, out_snd, out_rcv, dxt, dxr, ps, ga, gb,
     ld, w_s, w_r, wc_s, wc_r, x_s, x_r, sb_s, sb_r,
-    i_s, i_r, o_s, o_r, a_s, a_r, ac_s, ac_r, d_s, d_r, p_s, p_r, g_s, g_r,
+    i_s, i_r, ox_s, ox_r, o_s, o_r, a_s, a_r, ax_s, ax_r, ac_s, ac_r, d_s, d_r, p_s, p_r, g_s, g_r,
 ):
     dp = lax.axis_index("dp")
     mp = lax.axis_index("mp")
@@ -280,17 +280,6 @@
     gp2[0] = gp
     send(gp2.at[0], gp2.at[1], sb_s.at[2], sb_r.at[2], sibling)
 
-    def dx_body(j, _):
-        w = wf[pl.ds(4 * j, 4)].reshape(384, 512)
-        dxt[pl.ds(2 * j, 2)] = dot_t(w, gp2[0]).astype(BF16).reshape(2, 192, 128)
-        return 0
-
-    lax.fori_loop(0, 8, dx_body, 0)
-    mp_peers = [(b, k) for k in (4, 3, 5, 2, 6, 1, 7, 0) for b in range(2) if (b, k) != (0, 0)]
-    for b, k in mp_peers:
-        i = b * 8 + k
-        send(dxt.at[mpi(half_l(b), z + k)], dxr.at[i], d_s, d_r, on_mp(half_l(b), z + k))
-
     remote(jt.at[1], jt.at[2], sb_s.at[1], sb_r.at[1], sibling).wait_recv()
     remote(xg.at[:, 192:384], dys, sb_s.at[0], sb_r.at[0], sibling).wait_recv()
     jt_cat = jnp.concatenate([jt[0], jt[2]], axis=1)
@@ -299,10 +288,23 @@
         own = xg[pl.ds(2 * j, 2), 192:384, :].reshape(384, 128)
         other = dys[pl.ds(2 * j, 2)].reshape(384, 128)
         t = dot_t(jt_cat, jnp.concatenate([own, other], axis=1))
-        ot[pl.ds(2 * j, 2)] = t.reshape(2, 64, 384)
+        ot[pl.ds(2 * j, 2)] = t.astype(BF16).reshape(2, 64, 384)
         return 0
 
     lax.fori_loop(0, 8, ot_body, 0)
+
+    far_first = (4, 3, 5, 2, 6, 1, 7, 0)
+    near_first = (1, 7, 2, 6, 3, 5, 4)
+    for k in far_first:
+        send(ot.at[wrap(y + k) * 2 + 1 - h], out_x.at[k], ox_s, ox_r.at[k], y_near[2])
+
+    def out_pass(ks):
+        for k in ks:
+            remote(ot.at[0], out_x.at[k], ox_s, ox_r.at[k], y_near[2]).wait_recv()
+            value = ot[wrap(y + k) * 2 + h].astype(F32) + out_x[k].astype(F32)
+            out_snd[k] = value.astype(BF16)
+            if k:
+                send(out_snd.at[k], out_rcv.at[k], o_s, o_r, on_dp(y + k, h, c))
 
     class Reduce:
         def __init__(self, term, snd, rcv, s, r, near):
@@ -342,24 +344,51 @@
         def partner(self):
             return self.arrived(7, self.pair)
 
-    def term_out(off, b):
-        return ot[wrap(y + off) * 2 + half_h(b)]
-
     def term_in(off, b):
         i = wrap(y + off) * 2 + half_h(b)
         return dot(jnp.concatenate([xt[i, c], xts[i]], axis=1), gp2[...].reshape(256, 512))
 
-    ring_out = Reduce(term_out, out_snd, out_rcv, o_s, o_r, y_near)
     ring_in = Reduce(term_in, in_snd, in_rcv, i_s, i_r, y_near)
 
-    ring_out.step(0)
     remote(gp2.at[0], gp2.at[1], sb_s.at[2], sb_r.at[2], sibling).wait_recv()
     remote(xt.at[:, 1 - c], xts, sb_s.at[3], sb_r.at[3], sibling).wait_recv()
     ring_in.step(0)
-    for st in range(1, 4):
-        ring_out.step(st)
-        ring_in.step(st)
-    out_sum = ring_out.finish()
+
+    def dx_body(j, _):
+        w = wf[pl.ds(4 * j, 4)].reshape(384, 512)
+        dxt[pl.ds(2 * j, 2)] = dot_t(w, gp2[0]).astype(BF16).reshape(2, 192, 128)
+        return 0
+
+    lax.fori_loop(0, 8, dx_body, 0)
+    mp_peers = [(b, k) for k in (4, 3, 5, 2, 6, 1, 7, 0) for b in range(2) if (b, k) != (0, 0)]
+    for b, k in mp_peers:
+        i = b * 8 + k
+        send(dxt.at[mpi(half_l(b), z + k)], dxr.at[i], d_s, d_r, on_mp(half_l(b), z + k))
+
+    out_pass(far_first[:6])
+    ring_in.step(1)
+    out_pass(far_first[6:])
+    ring_in.step(2)
+
+    def out_block(yy, hh):
+        rows = pl.ds(pl.multiple_of(c * 128 + hh * 64, 64), 64)
+        return gwo_ref.at[rows, pl.ds(pl.multiple_of(wrap(yy) * 384, 128), 384)]
+
+    def halves(yy):
+        cols = pl.ds(pl.multiple_of(wrap(yy) * 384, 128), 384)
+        return [gwo_ref.at[pl.ds(pl.multiple_of(c * 128 + h * 64 + 32 * i, 32), 32), cols] for i in range(2)]
+
+    wait_bytes(out_rcv.at[1:8], o_r)
+    out_sum = out_snd[0].astype(F32)
+    for k in range(1, RING):
+        out_sum = out_sum + out_rcv[k].astype(F32)
+    own_out = out_block(y, h)
+    own_out[...] = (out_sum * FACTOR).astype(BF16)
+    for k in (1, 7, 2, 6):
+        send(own_out, own_out, a_s, a_r.at[k], on_dp(y + k, h, c))
+    send(own_out, own_out, ax_s, ax_r.at[0], y_near[2])
+    send(own_out, own_out, ac_s, ac_r, sibling)
+
 
     dxn = dxt[mp].astype(F32)
     wait_bytes(dxr.at[1:16], d_r)
@@ -384,26 +413,29 @@
     for i, p in enumerate(quad):
         send(ga.at[0], ga.at[i + 1], g_s.at[0], g_r.at[0], p)
 
-    def out_block(yy, hh):
-        rows = pl.ds(pl.multiple_of(c * 128 + hh * 64, 64), 64)
-        return gwo_ref.at[rows, pl.ds(pl.multiple_of(wrap(yy) * 384, 128), 384)]
-
-    def blk_out(off, b):
-        return out_block(y + off, half_h(b))
-
-    out_block(y, h)[...] = ((out_sum + ring_out.partner()) * FACTOR).astype(BF16)
-    ga_ring = Gather(blk_out, a_s, a_r, y_near, forward=(ac_s, ac_r))
-    ga_ring.start()
-
-    in_sum = ring_in.finish()
-    ga_ring.start_partner()
+    ring_in.step(3)
 
     wait_bytes(ga.at[1:4], g_r.at[0])
     gb[0] = (ga[0] + ga[1]) + (ga[2] + ga[3])
     for k in range(1, RING):
         send(gb.at[0], gb.at[k], g_s.at[1], g_r.at[1], on_dp(y + k, h, c))
 
-    step_rings((ga_ring,), 1)
+    for k in (1, 7, 2, 6, 3, 5, 4):
+        ref = out_block(y - k, h)
+        if k == 4:
+            for i, part in enumerate(halves(y - k)):
+                remote(part, part, a_s, a_r.at[(4, 0)[i]], sibling).wait_recv()
+        else:
+            remote(ref, ref, a_s, a_r.at[k], sibling).wait_recv()
+        if k in (2, 6):
+            turn = 1 if k == 2 else -1
+            part = halves(y - k)[(2, 6).index(k)]
+            send(ref, ref, a_s, a_r.at[k + turn], on_dp(y + turn, h, c))
+            send(part, part, a_s, a_r.at[(4, 0)[(2, 6).index(k)]], on_dp(y + 2 * turn, h, c))
+        send(ref, ref, ax_s, ax_r.at[k], y_near[2])
+        send(ref, ref, ac_s, ac_r, sibling)
+
+    in_sum = ring_in.finish()
 
     acc = ps[0]
     wait_bytes(ps.at[1:16], p_r)
@@ -413,21 +445,23 @@
     cot_own = xg[mp, 192:384, :].astype(F32)
     gx_ref[...] = (cot_own + x_inv * (scaled - mean0 - hat * mean1)).astype(BF16)
 
-    step_rings((ga_ring,), 2)
+    for k in (0,) + near_first:
+        ref = out_block(y - k, 1 - h)
+        remote(ref, ref, ax_s, ax_r.at[k], y_near[2]).wait_recv()
+        send(ref, ref, ac_s, ac_r, sibling)
+
     gwi_ref[...] = ((in_sum + ring_in.partner()) * FACTOR).astype(BF16)
-    step_rings((ga_ring,), 3)
     total = gb[0]
     wait_bytes(gb.at[1:8], g_r.at[1])
     for k in range(1, RING):
         total = total + gb[k]
     gs_ref[...] = total * FACTOR
-    step_rings((ga_ring,), 4)
-    wait_bytes(out_snd.at[0:16], ac_r)
+    wait_bytes(ot.at[0:16], ac_r)
 
     for ref, sem in (
         (xg.at[0:15], x_s), (wf.at[0:15], w_s), (wf.at[0:16], wc_s),
         (dys, sb_s.at[0]), (jt.at[1], sb_s.at[1]), (gp2.at[0], sb_s.at[2]), (xts, sb_s.at[3]),
-        (in_snd.at[0:15], i_s), (out_snd.at[0:15], o_s), (out_snd.at[0:15], a_s), (out_snd.at[0:16], ac_s),
+        (in_snd.at[0:15], i_s), (ot.at[0:8], ox_s), (ot.at[0:7], o_s), (ot.at[0:7], a_s), (ot.at[0:8], ax_s), (ot.at[0:16], ac_s),
         (dxt.at[0:15], d_s), (ps.at[0:15], p_s), (ga.at[0:3], g_s.at[0]), (gb.at[0:7], g_s.at[1]),
     ):
         wait_bytes(ref, sem)
@@ -447,14 +481,14 @@
         buf(16, 400, 128),
         buf(16, 2, 96, 128), buf(16, 96, 128),
         buf(16, 192, 128),
-        buf(16, 64, 384, dtype=F32),
+        buf(16, 64, 384),
         buf(3, 128, 128),
         buf(2, 128, 512),
-        buf(16, 96, 512), buf(16, 96, 512), buf(16, 64, 384), buf(16, 64, 384),
+        buf(16, 96, 512), buf(16, 96, 512), buf(8, 64, 384), buf(8, 64, 384), buf(8, 64, 384),
         buf(16, 192, 128), buf(16, 192, 128),
         buf(16, 8, 128, dtype=F32), buf(4, 8, 128, dtype=F32), buf(8, 8, 128, dtype=F32),
         dma((7,)), dma, dma((16,)), dma, dma, dma, dma((16,)), dma((4,)), dma((4,)),
-        dma, dma((16,)), dma, dma((16,)), dma, dma((16,)), dma, dma,
+        dma, dma((16,)), dma, dma((8,)), dma, dma, dma, dma((8,)), dma, dma((8,)), dma, dma,
         dma, dma, dma, dma, dma((2,)), dma((2,)),
     ]
     args = (activations.T, cotangent.T, ln_gain, w_in, w_out, q_gain, k_gain)

time: 96.6 us -> 89.3 us (0.924)
  Pallas kernels: 92.4 us -> 85.1 us
    pallas_call x1, Pallas kernels: 92.4 us -> 85.1 us  [per_device(): pl.pallas_call(kernel, out_shape=(jax.ShapeDtypeStruct((192, 128), BF16),...]
where the time goes in v3:
time: 89.3 us; the launch traced here: 89.2 us
  Pallas kernels  85.1 us (95%)
  local copies, waits for them, and re-layouts  2.92 us (3%)
    pallas_call x1, Pallas kernels, per_device(): pl.pallas_call(kernel, out_shape=(jax.ShapeDtypeStruct((192, 128), BF16),...  85.1 us
    unnamed x3, local copies, waits for them, and re-layouts  2.4 us

profile of v3, /device:TPU:1, one launch (start us, length us, event | category | flops | bytes accessed | tf_op | source)
XLA Modules:
  0.0 89.2 jit_solution(11199512179784816252)
XLA Ops:
  0.6 85.1 %shard_map.118 = (bf16[192,128]{1,0:T(8,128)(2,1)S(1)}, bf16[96,512]{1,0:T(8,128)(2,1)S(1)}, bf16[256,3072]{1,0:T(8,128)(2,1)S(1)}, f32[8,128]{1,0:T(8,128)S(1)}) custom-call(bf16[192,128]{1,0:T(8,128)(2,1)} %bitcast.8, bf16[192,128]{1,0:T(8,128)(2,1)} %bitcast.9, bf16[192]{0:T(256)(128)(2,1)} %gain_h.1, bf16[96,512]{1,0:T(8,128)(2,1)} %win_h.1, ...), custom_call_target="tpu_custom_call" | custom-call | tf_op jit(solution)/shard_map/pallas_call | solution.py:495
  85.7 0.5 fusion
  86.2 0.6 pad_maximum_fusion
  86.8 0.6 copy.16
  87.4 0.6 copy.17
  88.1 1.1 %copy.18 = bf16[256,3072]{1,0:T(8,128)(2,1)} copy(bf16[256,3072]{1,0:T(8,128)(2,1)S(1)} %get-tuple-element.25) | data formatting | bytes 3145728
  (1 shorter events, 0.0 us)

commit v4 on v3

--- a/solution.py
+++ b/solution.py
@@ -56,7 +56,7 @@
 
 def kernel(
     act_h, cot_h, gain_h, win_h, wout_h, qg_h, kg_h,
-    gx_ref, gwi_ref, gwo_ref, gs_ref,
+    gx_ref, gwi_ref, gwo_ref, gln_ref, gq_ref, gk_ref,
     gain_v, wout, qg_v, kg_v,
     wf, xg, xt, xts, dys, ot, jt, gp2,
     in_snd, in_rcv, out_x, out_snd, out_rcv, dxt, dxr, ps, ga, gb,
@@ -455,7 +455,10 @@
     wait_bytes(gb.at[1:8], g_r.at[1])
     for k in range(1, RING):
         total = total + gb[k]
-    gs_ref[...] = total * FACTOR
+    total = total * FACTOR
+    gln_ref[...] = jnp.concatenate([total[2:3], total[3:4, 0:64]], axis=1).reshape(192)
+    gq_ref[...] = total[0:1]
+    gk_ref[...] = total[1:2]
     wait_bytes(ot.at[0:16], ac_r)
 
     for ref, sem in (
@@ -465,6 +468,15 @@
         (dxt.at[0:15], d_s), (ps.at[0:15], p_s), (ga.at[0:3], g_s.at[0]), (gb.at[0:7], g_s.at[1]),
     ):
         wait_bytes(ref, sem)
+
+
+def store(*refs):
+    sources, results, sem = refs[0:6], refs[6:12], refs[12]
+    copies = [pltpu.make_async_copy(a, b, sem.at[i]) for i, (a, b) in enumerate(zip(sources, results))]
+    for cp in copies:
+        cp.start()
+    for cp in copies:
+        cp.wait()
 
 
 def per_device(activations, cotangent, ln_gain, w_in, w_out, q_gain, k_gain):
@@ -492,21 +504,31 @@
         dma, dma, dma, dma, dma((2,)), dma((2,)),
     ]
     args = (activations.T, cotangent.T, ln_gain, w_in, w_out, q_gain, k_gain)
-    grad_x, grad_w_in, grad_w_out, sums = pl.pallas_call(
+    shapes = (
+        jax.ShapeDtypeStruct((192, 128), BF16),
+        jax.ShapeDtypeStruct((96, 512), BF16),
+        jax.ShapeDtypeStruct((256, 3072), BF16),
+        jax.ShapeDtypeStruct((192,), F32),
+        jax.ShapeDtypeStruct((1, 128), F32),
+        jax.ShapeDtypeStruct((1, 128), F32),
+    )
+    results = pl.pallas_call(
         kernel,
-        out_shape=(
-            jax.ShapeDtypeStruct((192, 128), BF16),
-            jax.ShapeDtypeStruct((96, 512), BF16),
-            jax.ShapeDtypeStruct((256, 3072), BF16),
-            jax.ShapeDtypeStruct((8, 128), F32),
-        ),
+        out_shape=shapes,
         in_specs=[hbm] * 7,
-        out_specs=(vmem,) * 4,
+        out_specs=(vmem,) * 6,
         scratch_shapes=scratch,
         compiler_params=pltpu.CompilerParams(collective_id=0, has_side_effects=True, vmem_limit_bytes=48 << 20),
     )(*(pltpu.with_memory_space_constraint(a, pltpu.HBM) for a in args))
-    grad_ln = jnp.concatenate([sums[2], sums[3, 0:64]])
-    return grad_x.T, grad_w_in, grad_w_out, grad_ln, sums[0:1], sums[1:2]
+    grad_x, grad_w_in, grad_w_out, grad_ln, grad_q, grad_k = pl.pallas_call(
+        store,
+        out_shape=shapes,
+        in_specs=[pl.BlockSpec(memory_space=pl.ANY)] * 6,
+        out_specs=(hbm,) * 6,
+        scratch_shapes=[dma((6,))],
+        compiler_params=pltpu.CompilerParams(vmem_limit_bytes=1 << 20),
+    )(*results)
+    return grad_x.T, grad_w_in, grad_w_out, grad_ln, grad_q, grad_k
 
 
 def solution(mesh):

time: 89.3 us -> 87.1 us (0.975)
  local copies, waits for them, and re-layouts: 2.92 us -> 0 us
  Pallas kernels: 85.1 us -> 86.3 us
    unnamed x3 -> x0, local copies, waits for them, and re-layouts: 2.4 us -> none
    pallas_call x1 -> x2, Pallas kernels: 85.1 us -> 86.3 us  [the longest x1 85.1 us: per_device(): pl.pallas_call(kernel, out_shape=shapes, in_specs=[hbm] * 7, out_specs=(v...]
where the time goes in v4:
time: 87.1 us; the launch traced here: 87 us
  Pallas kernels  86.3 us (99%)
    pallas_call x1, Pallas kernels, per_device(): pl.pallas_call(kernel, out_shape=shapes, in_specs=[hbm] * 7, out_specs=(v...  85.1 us

profile of v4, /device:TPU:1, one launch (start us, length us, event | category | flops | bytes accessed | tf_op | source)
XLA Modules:
  0.0 87.0 jit_solution(3910185728938592331)
XLA Ops:
  0.6 85.1 %shard_map.118 = (bf16[192,128]{1,0:T(8,128)(2,1)S(1)}, bf16[96,512]{1,0:T(8,128)(2,1)S(1)}, bf16[256,3072]{1,0:T(8,128)(2,1)S(1)}, f32[192]{0:T(256)S(1)}, f32[1,128]{1,0:T(1,128)S(1)}, /*index=5*/f32[1,128]{1,0:T(1,128)S(1)}) custom-call(bf16[192,128]{1,0:T(8,128)(2,1)} %bitcast.3, bf16[192,128]{1,0:T(8,128)(2,1)} %bitcast.4, bf16[192]{0:T(256)(128)(2,1)} %gain_h.1, ...), custom_call_target="tpu_custom_call" | custom-call | tf_op jit(solution)/shard_map/pallas_call | solution.py:515
  85.7 1.3 %shard_map.119 = (bf16[192,128]{1,0:T(8,128)(2,1)}, bf16[96,512]{1,0:T(8,128)(2,1)}, bf16[256,3072]{1,0:T(8,128)(2,1)}, f32[192]{0:T(256)}, f32[1,128]{1,0:T(1,128)}, /*index=5*/f32[1,128]{1,0:T(1,128)}) custom-call(bf16[192,128]{1,0:T(8,128)(2,1)S(1)} %get-tuple-element.18.refs_0_, bf16[96,512]{1,0:T(8,128)(2,1)S(1)} %get-tuple-element.19.refs_1_, ...), custom_call_target="tpu_custom_call" | custom-call | tf_op jit(solution)/shard_map/pallas_call | solution.py:523
